TPU v7x, 32 devices: a whole 2x2x4 slice. The times are simulated.
32 devices in a mesh: group: 2 (over x), adapter: 16 (over z, y, core).
Axes of the slice: x: 2, y: 2, z: 4, core: 2. Of those that a mesh axis runs over, the one named last changes fastest.
Arguments:
- hidden: bfloat16 [4096, 8192], P(('group', 'adapter')), parts along dimension 0, may hold values from -6 to 6
- base_qkv: bfloat16 [4096, 10240], P(('group', 'adapter')), parts along dimension 0, may hold values from -6 to 6
- adapter_id: int32 [4096, 1], P(('group', 'adapter')), parts along dimension 0, may hold values from 0 to 15; in each aligned block of 128 rows (0 to 127, 128 to 255, ...) at most 16 rows name the same one
- shrink: bfloat16 [16, 8192, 192], P('adapter'), may hold values from -0.0625 to 0.0625
- expand_q: bfloat16 [16, 64, 8192], P('adapter'), may hold values from -0.75 to 0.75
- expand_kv: bfloat16 [16, 2, 64, 1024], P('adapter'), may hold values from -0.75 to 0.75
Outputs:
- qkv: bfloat16 [4096, 10240], P(('group', 'adapter')), parts along dimension 0
There are 2 independent parts, one for each index of `group`. A program takes and returns all parts, laid end to end along the dimension named above; an argument that names none is the same for every part. Nothing has to cross between parts.
Inputs may be any that keep to these rules, and one draw needn't show every extreme that they name: `adapter_id`: within the rows of one device (aligned blocks of 128 rows) no adapter is named by more than 16 rows, and in some block one adapter is named by exactly 16 rows.
All inputs are finite; a program needn't handle non-finite values.
Results may differ from a plain program's by a relative error of at most 0.0052.
Values may be sent and summed in bfloat16 or wider, within the bound.
A program may use at most 64 MiB of HBM per device.

v0:
```python
import jax
import jax.numpy as jnp
from jax import lax
from jax.sharding import PartitionSpec as P

R = 64


def project(latent, weight):
    return jnp.einsum("sacr,are->sace", latent, weight, preferred_element_type=jnp.float32).astype(
        jnp.bfloat16
    )


def per_device(hidden, base_qkv, adapter_id, shrink, expand_q, expand_kv):
    peer_count = lax.axis_size("adapter")
    row_count = hidden.shape[0]
    owned_count = shrink.shape[0]
    model_width = hidden.shape[1]
    slot_cap = max(2, (2 * row_count + peer_count * owned_count - 1) // (peer_count * owned_count))
    row_adapter = adapter_id[:, 0]
    matches = (row_adapter[:, None] == row_adapter[None, :]).astype(jnp.int32)
    earlier = lax.broadcasted_iota(jnp.int32, (row_count, row_count), 0) < lax.broadcasted_iota(
        jnp.int32, (row_count, row_count), 1
    )
    rank_in = jnp.sum(matches * earlier.astype(jnp.int32), axis=0)
    slot_of = row_adapter * slot_cap + rank_in
    slot_count = peer_count * owned_count * slot_cap
    placer = (
        lax.broadcasted_iota(jnp.int32, (slot_count, row_count), 0) == slot_of[None, :]
    ).astype(jnp.bfloat16)
    outgoing = jnp.dot(placer, hidden, preferred_element_type=jnp.float32).astype(jnp.bfloat16)
    outgoing = outgoing.reshape(peer_count, owned_count, slot_cap, model_width)
    latent = jnp.einsum(
        "sacd,adr->sacr",
        lax.all_to_all(outgoing, "adapter", split_axis=0, concat_axis=0, tiled=True),
        shrink,
        preferred_element_type=jnp.float32,
    ).astype(jnp.bfloat16)
    query_delta = project(latent[..., 0:R], expand_q)
    key_delta = project(latent[..., R : 2 * R], expand_kv[:, 0])
    value_delta = project(latent[..., 2 * R : 3 * R], expand_kv[:, 1])
    joined = jnp.concatenate([query_delta, key_delta, value_delta], axis=3)
    returned = lax.all_to_all(joined, "adapter", split_axis=0, concat_axis=0, tiled=True)
    flattened = returned.reshape(slot_count, returned.shape[3])
    deltas = jnp.take(flattened, slot_of, axis=0)
    return (base_qkv.astype(jnp.float32) + deltas.astype(jnp.float32)).astype(jnp.bfloat16)


def solution(mesh):
    placed = (
        P(("group", "adapter"), None),
        P(("group", "adapter"), None),
        P(("group", "adapter"), None),
        P("adapter", None, None),
        P("adapter", None, None),
        P("adapter", None, None, None),
    )
    return jax.shard_map(
        per_device,
        mesh=mesh,
        in_specs=placed,
        out_specs=P(("group", "adapter"), None),
        check_vma=False,
    )
```

profile of v0, /device:TPU:15, one launch (start us, length us, event | category | flops | bytes accessed | tf_op | source)
XLA Modules:
  0.0 245.8 jit_solution(1960123111602990353)
XLA Ops:
  0.0 0.0 copy-start
  0.0 0.9 select_reduce_fusion
  0.9 0.7 multiply_add_fusion
  1.6 2.8 %convolution_convert_fusion.1 = bf16[256,8192]{1,0:T(8,128)(2,1)S(1)} fusion(bf16[128,8192]{1,0:T(8,128)(2,1)} %param.6, s32[128]{0:T(128)S(1)} %multiply_add_fusion), kind=kOutput, calls=%fused_computation.2 | convolution fusion | flops 539000832 | bytes 6291968 | tf_op jit(solution)/shard_map/dot_general | solution.py:32
  4.5 98.6 %all_to_all.10 = bf16[16,1,16,8192]{3,2,1,0:T(8,128)(2,1)S(1)} all-to-all(bf16[16,1,16,8192]{3,2,1,0:T(8,128)(2,1)S(1)} %bitcast.79), channel_id=1, replica_groups=mesh['group'=2,'adapter'=16] {'adapter'}, dimensions={0} | all-to-all | bytes 8388608 | tf_op jit(solution)/shard_map/all_to_all | solution.py:36
  103.1 0.0 copy-done
  103.1 0.0 copy-start.2
  103.1 0.0 copy-start.1
  103.1 1.5 fusion.11
  104.6 0.0 copy-done.2
  104.6 0.3 fusion.4
  105.0 0.3 fusion.5
  105.2 0.0 copy-done.1
  105.2 1.2 fusion
  106.5 4.8 %maximum_bitcast_fusion = bf16[16,1,16,10240]{3,2,1,0:T(8,128)(2,1)} fusion(bf16[16,1,16,1024]{3,2,0,1:T(8,128)(2,1)S(1)} %fusion.5, bf16[16,1,16,1024]{3,2,0,1:T(8,128)(2,1)S(1)} %fusion.4, bf16[16,1,16,8192]{3,2,0,1:T(8,128)(2,1)S(1)} %fusion), kind=kLoop, calls=%fused_computation.4 | loop fusion | flops 15728640 | bytes 10485760 | tf_op jit(solution)/shard_map/concatenate | solution.py:43
  111.3 0.0 copy-start.3
  111.3 5.4 %all-to-all-start.1 = ((bf16[16,1,16,10240]{3,2,1,0:T(8,128)(2,1)}), bf16[16,1,16,10240]{3,2,1,0:T(8,128)(2,1)}, u32[]{:S(2)}, u32[]{:S(2)}) async-start(bf16[16,1,16,10240]{3,2,1,0:T(8,128)(2,1)} %maximum_bitcast_fusion), calls=%async_computation.1 | async-start | bytes 10485760 | tf_op jit(solution)/shard_map/all_to_all | solution.py:44
  116.8 0.0 copy-done.3
  116.8 114.9 %all-to-all-done.1 = bf16[16,1,16,10240]{3,2,1,0:T(8,128)(2,1)} async-done(((bf16[16,1,16,10240]{3,2,1,0:T(8,128)(2,1)}), bf16[16,1,16,10240]{3,2,1,0:T(8,128)(2,1)}, u32[]{:S(2)}, u32[]{:S(2)}) %all-to-all-start.1) | async-done | bytes 5242912 | tf_op jit(solution)/shard_map/all_to_all | solution.py:44
  231.7 9.2 %gather_fusion = bf16[128,10240]{1,0:T(8,128)(2,1)} fusion(bf16[256,10240]{1,0:T(8,128)(2,1)} %bitcast.32, s32[1024]{0:T(1024)S(1)} %pad_clamp_fusion), kind=kCustom, calls=%fused_computation | custom fusion | bytes 5243392 | tf_op jit(solution)/shard_map/jit(_take)/gather | solution.py:46
  240.9 4.9 %add_convert_fusion = bf16[128,10240]{1,0:T(8,128)(2,1)} fusion(bf16[128,10240]{1,0:T(8,128)(2,1)} %param.7, bf16[128,10240]{1,0:T(8,128)(2,1)} %gather_fusion, pred[128]{0:T(512)(128)(4,1)S(1)} %get-tuple-element.5), kind=kLoop, calls=%fused_computation.5 | loop fusion | flops 6553600 | bytes 7864448 | tf_op jit(solution)/shard_map/convert_element_type | solution.py:47
  (2 shorter events, 0.0 us)
Async XLA Ops:
  0.0 103.1 %copy-start = (bf16[1,8192,192]{1,2,0:T(8,128)(2,1)S(1)}, bf16[1,8192,192]{1,2,0:T(8,128)(2,1)}, u32[]{:S(2)}) copy-start(bf16[1,8192,192]{1,2,0:T(8,128)(2,1)} %param.9) | copy-start | bytes 9437188
  103.1 1.5 copy-start.2
  103.1 2.2 copy-start.1
  111.3 5.5 %copy-start.3 = (s32[128,1]{0,1:T(1,128)S(1)}, s32[128,1]{0,1:T(1,128)}, u32[]{:S(2)}) copy-start(s32[128,1]{0,1:T(1,128)} %param.8) | copy-start | bytes 1540
  111.3 120.4 %all-to-all-start.1 = ((bf16[16,1,16,10240]{3,2,1,0:T(8,128)(2,1)}), bf16[16,1,16,10240]{3,2,1,0:T(8,128)(2,1)}, u32[]{:S(2)}, u32[]{:S(2)}) async-start(bf16[16,1,16,10240]{3,2,1,0:T(8,128)(2,1)} %maximum_bitcast_fusion), calls=%async_computation.1 | async-start | bytes 10485760 | tf_op jit(solution)/shard_map/all_to_all | solution.py:44
where the time goes:
time: 246 us
  waiting for transfers between devices  115 us (47%)
  blocking collectives  98.6 us (40%)
  other arithmetic  11.4 us (5%)
  local copies, waits for them, and re-layouts  9.19 us (4%)
  matrix products  6.18 us (3%)
  starting transfers between devices  5.45 us (2%)
    all_to_all x1, waiting for transfers between devices, per_device(): lax.all_to_all(joined, 'adapter', split_axis=0, concat_axis=0, tiled=True)  115 us
    all_to_all x1, blocking collectives, per_device(): lax.all_to_all(outgoing, 'adapter', split_axis=0, concat_axis=0, tiled=True)  98.6 us
    gather x1, local copies, waits for them, and re-layouts, per_device(): deltas = jnp.take(flattened, slot_of, axis=0)  9.17 us
    all_to_all x1, starting transfers between devices, per_device(): lax.all_to_all(joined, 'adapter', split_axis=0, concat_axis=0, tiled=True)  5.45 us
    convert_element_type x1, other arithmetic, per_device(): (base_qkv.astype(jnp.float32) + deltas.astype(jnp.float32)).astype(jnp.bf...  4.94 us
  transfers between devices with their start and end apart: 1, of which 1 were waited for; matrix products, arithmetic and copies ran while one was open for 0% of the time, Pallas kernels for 0%

commit v1 on v0

--- a/solution.py
+++ b/solution.py
@@ -1,6 +1,8 @@
 import jax
 import jax.numpy as jnp
 from jax import lax
+from jax.experimental import pallas as pl
+from jax.experimental.pallas import tpu as pltpu
 from jax.sharding import PartitionSpec as P
 
 R = 64
@@ -47,6 +49,290 @@
     return (base_qkv.astype(jnp.float32) + deltas.astype(jnp.float32)).astype(jnp.bfloat16)
 
 
+Z, Y, C = 4, 2, 2
+PEERS = Z * Y * C
+ROW_DEV = 128
+CAP = 16
+D = 8192
+KVW = 1024
+QKV = D + 2 * KVW
+HALF = R // 2
+SLOTS = PEERS * CAP
+MESH = pl.DeviceIdType.MESH
+
+
+def exchange(
+    id_row, id_col, hidden, base, shrink, expand_q, expand_kv, out,
+    wg, outgoing, incoming, shrink_v, base_v, acc, lat_out, lat_in, lat3,
+    local_sem, p_send, p_recv, l_send, l_recv, w_recv, z_send, y_send, x_send, c_send,
+):
+    x = lax.axis_index("group")
+    me = lax.axis_index("adapter")
+    z, y, c = me // 4, (me // 2) % 2, me % 2
+
+    def index(zz, yy, cc):
+        return zz * 4 + yy * 2 + cc
+
+    own_rows = pl.ds(pl.multiple_of(me * R, R), R)
+    loads = [
+        pltpu.make_async_copy(expand_q.at[0], wg.at[own_rows, 0:D], local_sem.at[0]),
+        pltpu.make_async_copy(expand_kv.at[0, 0], wg.at[own_rows, D : D + KVW], local_sem.at[1]),
+        pltpu.make_async_copy(expand_kv.at[0, 1], wg.at[own_rows, D + KVW : QKV], local_sem.at[2]),
+        pltpu.make_async_copy(shrink.at[0], shrink_v, local_sem.at[3]),
+        pltpu.make_async_copy(base, base_v, local_sem.at[4]),
+    ]
+    for load in loads:
+        load.start()
+
+    barrier = pltpu.get_barrier_semaphore()
+    for k in range(1, PEERS):
+        pl.semaphore_signal(barrier, inc=1, device_id=(x, (me + k) % PEERS), device_id_type=MESH)
+    pl.semaphore_signal(barrier, inc=1, device_id=(1 - x, me), device_id_type=MESH)
+    pl.semaphore_wait(barrier, PEERS)
+
+    def piece(a, h):
+        return wg.at[pl.ds(pl.multiple_of(a * R + h * HALF, HALF), HALF), :]
+
+    def push(a, h, target, sem):
+        return pltpu.make_async_remote_copy(
+            src_ref=piece(a, h), dst_ref=piece(a, h), send_sem=sem, recv_sem=w_recv.at[a, h],
+            device_id=target, device_id_type=MESH,
+        )
+
+    def to_up(zz):
+        return push(index(zz, y, c), x, (x, index(z + 1, y, c)), z_send.at[zz, 0])
+
+    def to_down(zz):
+        return push(index(zz, y, c), x, (x, index(z - 1, y, c)), z_send.at[zz, 1])
+
+    def to_y(zz):
+        return push(index(zz, y, c), x, (x, index(z, 1 - y, c)), y_send.at[zz])
+
+    def to_x(zz, yy):
+        return push(index(zz, yy, c), x, (1 - x, me), x_send.at[zz, yy])
+
+    def to_core(zz, yy, h):
+        return push(index(zz, yy, c), h, (x, index(z, y, 1 - c)), c_send.at[zz, yy, h])
+
+    def arrived(a, h):
+        push(a, h, (x, me), c_send.at[0, 0, 0]).wait_recv()
+
+    for load in loads[0:3]:
+        load.wait()
+
+    @pl.when(z < Z - 1)
+    def _():
+        to_up(z).start()
+
+    @pl.when(z > 0)
+    def _():
+        to_down(z).start()
+
+    to_y(z).start()
+    to_core(z, y, 0).start()
+    to_core(z, y, 1).start()
+
+    ids_row, ids_col = id_row[...], id_col[...]
+    matches = ids_col == ids_row
+    first = lax.broadcasted_iota(jnp.int32, (ROW_DEV, ROW_DEV), 0)
+    second = lax.broadcasted_iota(jnp.int32, (ROW_DEV, ROW_DEV), 1)
+    rank_row = jnp.sum(jnp.where(matches & (first < second), 1, 0), axis=0, keepdims=True)
+    rank_col = jnp.sum(jnp.where(matches & (second < first), 1, 0), axis=1, keepdims=True)
+    slot_row, slot_col = ids_row * CAP + rank_row, ids_col * CAP + rank_col
+    placer = jnp.where(
+        lax.broadcasted_iota(jnp.int32, (SLOTS, ROW_DEV), 0) == slot_row, 1.0, 0.0
+    ).astype(jnp.bfloat16)
+    taker = jnp.where(
+        lax.broadcasted_iota(jnp.int32, (ROW_DEV, SLOTS), 1) == slot_col, 1.0, 0.0
+    ).astype(jnp.bfloat16)
+
+    @pl.loop(0, D // 1024)
+    def _(step):
+        columns = pl.ds(pl.multiple_of(step * 1024, 1024), 1024)
+        outgoing[:, columns] = jnp.dot(
+            placer, hidden[:, columns], preferred_element_type=jnp.float32
+        ).astype(jnp.bfloat16)
+
+    def block(ref, device):
+        return ref.at[pl.ds(pl.multiple_of(device * CAP, CAP), CAP), :]
+
+    def row_copy(k):
+        peer = (me + k) % PEERS
+        return pltpu.make_async_remote_copy(
+            src_ref=block(outgoing, peer), dst_ref=block(incoming, me),
+            send_sem=p_send.at[k], recv_sem=p_recv.at[k], device_id=(x, peer), device_id_type=MESH,
+        )
+
+    def latent_copy(k):
+        peer = (me + k) % PEERS
+        return pltpu.make_async_remote_copy(
+            src_ref=block(lat_out, peer), dst_ref=block(lat_in, me),
+            send_sem=l_send.at[k], recv_sem=l_recv.at[k], device_id=(x, peer), device_id_type=MESH,
+        )
+
+    own = pltpu.make_async_copy(block(outgoing, me), block(incoming, me), local_sem.at[5])
+    own.start()
+    for k in ORDER:
+        row_copy(k).start()
+
+    for distance in range(1, Z):
+        for up in (0, 1):
+            zz = z - distance if up else z + distance
+            inside = zz >= 0 if up else zz < Z
+            more = z < Z - 1 if up else z > 0
+
+            @pl.when(inside)
+            def _(zz=zz, more=more, up=up):
+                arrived(index(zz, y, c), x)
+
+                @pl.when(more)
+                def _():
+                    (to_up if up else to_down)(zz).start()
+
+                to_y(zz).start()
+                to_x(zz, y).start()
+                to_core(zz, y, x).start()
+
+    for turn in range(Z):
+        zz = (z + turn) % Z
+        arrived(index(zz, 1 - y, c), x)
+        to_x(zz, 1 - y).start()
+        to_core(zz, 1 - y, x).start()
+
+    for turn in range(Z):
+        zz = (z + turn) % Z
+        for yy in (y, 1 - y):
+            if turn == 0 and yy is y:
+                continue
+            arrived(index(zz, yy, c), 1 - x)
+            to_core(zz, yy, 1 - x).start()
+
+    loads[3].wait()
+    own.wait()
+    for k in range(1, PEERS):
+        row_copy(k).wait_recv()
+
+    acc[...] = jnp.zeros_like(acc)
+
+    @pl.loop(0, D // 1024)
+    def _(step):
+        part = pl.ds(pl.multiple_of(step * 1024, 1024), 1024)
+        acc[...] += jnp.dot(incoming[:, part], shrink_v[part, :], preferred_element_type=jnp.float32)
+
+    from_at = lax.broadcasted_iota(jnp.int32, (3 * R, 6 * R), 0)
+    to_at = lax.broadcasted_iota(jnp.int32, (3 * R, 6 * R), 1)
+    block_of = jnp.where(from_at >= R, 1, 0) + jnp.where(from_at >= 2 * R, 1, 0)
+    spread = jnp.where(to_at == from_at + R * block_of + R * c, 1.0, 0.0).astype(jnp.bfloat16)
+    lat_out[...] = jnp.dot(
+        acc[...].astype(jnp.bfloat16), spread, preferred_element_type=jnp.float32
+    ).astype(jnp.bfloat16)
+
+    for k in range(1, PEERS):
+        latent_copy(k).start()
+    own_slots = pl.ds(pl.multiple_of(me * CAP, CAP), CAP)
+    lat_in[own_slots, :] = lat_out[own_slots, :]
+
+    for zz in range(Z):
+        for yy in range(Y):
+            for h in range(2):
+                arrived(index(zz, yy, 1 - c), h)
+    loads[4].wait()
+    for k in range(1, PEERS):
+        latent_copy(k).wait_recv()
+
+    for pair in range(PEERS // 2):
+        slots = slice(pair * 2 * CAP, (pair + 1) * 2 * CAP)
+        got = jnp.dot(taker[:, slots], lat_in[slots, :], preferred_element_type=jnp.float32).astype(jnp.bfloat16)
+        for which in range(3):
+            lat3[which, :, pair * 128 : (pair + 1) * 128] = got[:, which * 128 : (which + 1) * 128]
+
+    def finish(which, columns):
+        delta = jnp.dot(lat3[which], wg[:, columns], preferred_element_type=jnp.float32).astype(jnp.bfloat16)
+        out[:, columns] = (base_v[:, columns].astype(jnp.float32) + delta.astype(jnp.float32)).astype(jnp.bfloat16)
+
+    @pl.loop(0, D // 512)
+    def _(step):
+        finish(0, pl.ds(pl.multiple_of(step * 512, 512), 512))
+
+    for which in (1, 2):
+
+        @pl.loop(0, KVW // 512)
+        def _(step, which=which):
+            finish(which, pl.ds(pl.multiple_of(D + (which - 1) * KVW + step * 512, 512), 512))
+
+    for k in range(1, PEERS):
+        row_copy(k).wait_send()
+        latent_copy(k).wait_send()
+    for zz in range(Z):
+
+        @pl.when((z < Z - 1) & (zz <= z))
+        def _(zz=zz):
+            to_up(zz).wait_send()
+
+        @pl.when((z > 0) & (zz >= z))
+        def _(zz=zz):
+            to_down(zz).wait_send()
+
+        to_y(zz).wait_send()
+        for yy in range(Y):
+            for h in range(2):
+                to_core(zz, yy, h).wait_send()
+
+            @pl.when((zz != z) | (yy != y))
+            def _(zz=zz, yy=yy):
+                to_x(zz, yy).wait_send()
+
+
+ORDER = tuple(range(1, PEERS))
+
+
+def gathered(hidden, base_qkv, adapter_id, shrink, expand_q, expand_kv):
+    dma = pltpu.SemaphoreType.DMA
+    vmem, anywhere = pl.BlockSpec(memory_space=pltpu.VMEM), pl.BlockSpec(memory_space=pl.ANY)
+    bf16 = jnp.bfloat16
+    return pl.pallas_call(
+        exchange,
+        out_shape=jax.ShapeDtypeStruct((ROW_DEV, QKV), bf16),
+        in_specs=[vmem, vmem, vmem, anywhere, anywhere, anywhere, anywhere],
+        out_specs=vmem,
+        scratch_shapes=[
+            pltpu.VMEM((PEERS * R, QKV), bf16),
+            pltpu.VMEM((SLOTS, D), bf16),
+            pltpu.VMEM((SLOTS, D), bf16),
+            pltpu.VMEM((D, 3 * R), bf16),
+            pltpu.VMEM((ROW_DEV, QKV), bf16),
+            pltpu.VMEM((SLOTS, 3 * R), jnp.float32),
+            pltpu.VMEM((SLOTS, 6 * R), bf16),
+            pltpu.VMEM((SLOTS, 6 * R), bf16),
+            pltpu.VMEM((3, ROW_DEV, PEERS * R), bf16),
+            dma((6,)),
+            dma((PEERS,)),
+            dma((PEERS,)),
+            dma((PEERS,)),
+            dma((PEERS,)),
+            dma((PEERS, 2)),
+            dma((Z, 2)),
+            dma((Z,)),
+            dma((Z, Y)),
+            dma((Z, Y, 2)),
+        ],
+        compiler_params=pltpu.CompilerParams(
+            collective_id=0, has_side_effects=True, vmem_limit_bytes=56 * 1024 * 1024
+        ),
+        cost_estimate=pl.CostEstimate(flops=4 * 10**9, bytes_accessed=12 * 10**6, transcendentals=0),
+    )(adapter_id.reshape(1, ROW_DEV), adapter_id, hidden, base_qkv, shrink, expand_q, expand_kv)
+
+
+def fits(mesh, hidden, shrink, expand_q):
+    groups, peers = mesh.shape["group"], mesh.shape["adapter"]
+    return (
+        (groups, peers) == (2, PEERS)
+        and hidden.shape == (groups * peers * ROW_DEV, D)
+        and shrink.shape == (PEERS, D, 3 * R)
+        and expand_q.shape == (PEERS, R, D)
+    )
+
+
 def solution(mesh):
     placed = (
         P(("group", "adapter"), None),
@@ -56,10 +342,16 @@
         P("adapter", None, None),
         P("adapter", None, None, None),
     )
-    return jax.shard_map(
-        per_device,
+
+    def whole(hidden, base_qkv, adapter_id, shrink, expand_q, expand_kv):
+        body = gathered if fits(mesh, hidden, shrink, expand_q) else per_device
+        return mapped(body)(hidden, base_qkv, adapter_id, shrink, expand_q, expand_kv)
+
+    mapped = lambda body: jax.shard_map(
+        body,
         mesh=mesh,
         in_specs=placed,
         out_specs=P(("group", "adapter"), None),
         check_vma=False,
     )
+    return whole

time: 246 us -> 242 us (0.984)
  the two profiles are of different devices: /device:TPU:15 before, /device:TPU:0 now
where the time goes in v1:
time: 242 us; the launch traced here: 241 us
  Pallas kernels  230 us (95%)
  local copies, waits for them, and re-layouts  10.8 us (4%)
    pallas_call x1, Pallas kernels, gathered(): pl.pallas_call(exchange, out_shape=jax.ShapeDtypeStruct((ROW_DEV, QKV), b...  230 us
    unnamed x3, local copies, waits for them, and re-layouts  10.8 us

profile of v1, /device:TPU:0, one launch (start us, length us, event | category | flops | bytes accessed | tf_op | source)
XLA Modules:
  0.0 241.2 jit_solution(9017353586478136025)
XLA Ops:
  0.0 1.4 copy.7.id_col
  1.4 5.9 %copy.8.shrink = bf16[1,8192,192]{2,1,0:T(8,128)(2,1)} copy(bf16[1,8192,192]{1,2,0:T(8,128)(2,1)} %param.9) | data formatting | bytes 6291456 | tf_op args[3]
  7.3 230.5 %shard_map.64 = bf16[128,10240]{1,0:T(8,128)(2,1)} custom-call(s32[1,128]{1,0:T(1,128)} %bitcast.1, s32[128,1]{1,0:T(8,128)} %copy.7.id_col, bf16[128,8192]{1,0:T(8,128)(2,1)} %hidden.1, bf16[128,10240]{1,0:T(8,128)(2,1)} %base.1, bf16[1,8192,192]{2,1,0:T(8,128)(2,1)} %copy.8.shrink, bf16[1,64,8192]{2,1,0:T(8,128)(2,1)} %expand_q.1, ...), custom_call_target="tpu_custom_call" | custom-call | flops 4000000000 | bytes 12000000 | tf_op jit(solution)/shard_map/pallas_call | solution.py:293
  237.8 3.5 %copy.10 = bf16[128,10240]{1,0:T(8,128)(2,1)} copy(bf16[128,10240]{1,0:T(8,128)(2,1)} %shard_map.64) | data formatting | bytes 5242880

commit v2 on v1

--- a/solution.py
+++ b/solution.py
@@ -62,13 +62,15 @@
 
 
 def exchange(
-    id_row, id_col, hidden, base, shrink, expand_q, expand_kv, out,
-    wg, outgoing, incoming, shrink_v, base_v, acc, lat_out, lat_in, lat3,
+    id_row, hidden, base, shrink, expand_q, expand_kv, out,
+    wg, outgoing, incoming, shrink_v, base_v, latents, lat_out, lat_in, lat3, total,
     local_sem, p_send, p_recv, l_send, l_recv, w_recv, z_send, y_send, x_send, c_send,
 ):
     x = lax.axis_index("group")
     me = lax.axis_index("adapter")
     z, y, c = me // 4, (me // 2) % 2, me % 2
+    at = me % 4
+    planes = (z, z + 1 - 2 * (z % 2), (z + 2) % 4, 3 - z)
 
     def index(zz, yy, cc):
         return zz * 4 + yy * 2 + cc
@@ -132,19 +134,25 @@
     to_core(z, y, 0).start()
     to_core(z, y, 1).start()
 
-    ids_row, ids_col = id_row[...], id_col[...]
-    matches = ids_col == ids_row
     first = lax.broadcasted_iota(jnp.int32, (ROW_DEV, ROW_DEV), 0)
     second = lax.broadcasted_iota(jnp.int32, (ROW_DEV, ROW_DEV), 1)
-    rank_row = jnp.sum(jnp.where(matches & (first < second), 1, 0), axis=0, keepdims=True)
-    rank_col = jnp.sum(jnp.where(matches & (second < first), 1, 0), axis=1, keepdims=True)
-    slot_row, slot_col = ids_row * CAP + rank_row, ids_col * CAP + rank_col
+    ids = id_row[...]
+    ids_col = jnp.sum(jnp.where(first == second, ids, 0), axis=1, keepdims=True)
+    rank = jnp.sum(jnp.where((ids_col == ids) & (first < second), 1, 0), axis=0, keepdims=True)
+    plane = sum(jnp.where(ids >= 4 * p, 1, 0) for p in range(1, Z))
+    place = sum(jnp.where(plane == planes[g], g, 0) for g in range(1, Z))
+    slot = place * (4 * CAP) + (ids - 4 * plane) * CAP + rank
+    slot_col = jnp.sum(jnp.where(first == second, slot, 0), axis=1, keepdims=True)
     placer = jnp.where(
-        lax.broadcasted_iota(jnp.int32, (SLOTS, ROW_DEV), 0) == slot_row, 1.0, 0.0
+        lax.broadcasted_iota(jnp.int32, (SLOTS, ROW_DEV), 0) == slot, 1.0, 0.0
     ).astype(jnp.bfloat16)
     taker = jnp.where(
         lax.broadcasted_iota(jnp.int32, (ROW_DEV, SLOTS), 1) == slot_col, 1.0, 0.0
     ).astype(jnp.bfloat16)
+    from_at = lax.broadcasted_iota(jnp.int32, (3 * R, 6 * R), 0)
+    to_at = lax.broadcasted_iota(jnp.int32, (3 * R, 6 * R), 1)
+    block_of = jnp.where(from_at >= R, 1, 0) + jnp.where(from_at >= 2 * R, 1, 0)
+    spread = jnp.where(to_at == from_at + R * block_of + R * c, 1.0, 0.0).astype(jnp.bfloat16)
 
     @pl.loop(0, D // 1024)
     def _(step):
@@ -153,29 +161,89 @@
             placer, hidden[:, columns], preferred_element_type=jnp.float32
         ).astype(jnp.bfloat16)
 
-    def block(ref, device):
-        return ref.at[pl.ds(pl.multiple_of(device * CAP, CAP), CAP), :]
-
-    def row_copy(k):
-        peer = (me + k) % PEERS
+    def block(ref, g, n):
+        return ref.at[pl.ds(pl.multiple_of((g * 4 + n) * CAP, CAP), CAP), :]
+
+    def peer_copy(source, landing, send, recv, g, j):
+        n = (at + j) % 2 + (at // 2 + j // 2) % 2 * 2
         return pltpu.make_async_remote_copy(
-            src_ref=block(outgoing, peer), dst_ref=block(incoming, me),
-            send_sem=p_send.at[k], recv_sem=p_recv.at[k], device_id=(x, peer), device_id_type=MESH,
+            src_ref=block(source, g, n), dst_ref=block(landing, g, at),
+            send_sem=send.at[g * 4 + j], recv_sem=recv.at[g * 4 + j],
+            device_id=(x, planes[g] * 4 + n), device_id_type=MESH,
         )
 
-    def latent_copy(k):
-        peer = (me + k) % PEERS
-        return pltpu.make_async_remote_copy(
-            src_ref=block(lat_out, peer), dst_ref=block(lat_in, me),
-            send_sem=l_send.at[k], recv_sem=l_recv.at[k], device_id=(x, peer), device_id_type=MESH,
-        )
-
-    own = pltpu.make_async_copy(block(outgoing, me), block(incoming, me), local_sem.at[5])
-    own.start()
-    for k in ORDER:
-        row_copy(k).start()
-
-    for distance in range(1, Z):
+    def row_copy(g, j):
+        return peer_copy(outgoing, incoming, p_send, p_recv, g, j)
+
+    def latent_copy(g, j):
+        return peer_copy(lat_out, lat_in, l_send, l_recv, g, j)
+
+    def others(g):
+        return [j for j in range(4) if (g, j) != (0, 0)]
+
+    def send_rows(g, near):
+        for j in others(g):
+            if (j < 2) == near:
+                row_copy(g, j).start()
+
+    def serve(g):
+        for j in others(g):
+            row_copy(g, j).wait_recv()
+        span = slice(g * 4 * CAP, (g + 1) * 4 * CAP)
+        latents[...] = jnp.zeros_like(latents)
+
+        @pl.loop(0, D // 1024)
+        def _(step):
+            part = pl.ds(pl.multiple_of(step * 1024, 1024), 1024)
+            latents[...] += lax.dot_general(
+                incoming[span, part], shrink_v[:, part], (((1,), (1,)), ((), ())),
+                preferred_element_type=jnp.float32,
+            )
+
+        lat_out[span, :] = jnp.dot(
+            latents[...].astype(jnp.bfloat16), spread, preferred_element_type=jnp.float32
+        ).astype(jnp.bfloat16)
+        for j in others(g):
+            latent_copy(g, j).start()
+        if g == 0:
+            own_slots = pl.ds(pl.multiple_of(at * CAP, CAP), CAP)
+            lat_in[own_slots, :] = lat_out[own_slots, :]
+
+    def add_plane(g):
+        for yy in range(Y):
+            for h in range(2):
+                arrived(index(planes[g], yy, 1 - c), h)
+        for j in others(g):
+            latent_copy(g, j).wait_recv()
+        for pair in range(2):
+            slots = slice((2 * g + pair) * 2 * CAP, (2 * g + pair + 1) * 2 * CAP)
+            got = jnp.dot(taker[:, slots], lat_in[slots, :], preferred_element_type=jnp.float32)
+            got = got.astype(jnp.bfloat16)
+            for which in range(3):
+                lat3[which, :, pair * 128 : (pair + 1) * 128] = got[:, which * 128 : (which + 1) * 128]
+        rows = pl.ds(pl.multiple_of(planes[g] * 4 * R, 4 * R), 4 * R)
+
+        def add(which, columns):
+            term = jnp.dot(lat3[which], wg[rows, columns], preferred_element_type=jnp.float32)
+            if g > 0:
+                term += total[:, columns]
+            if g < Z - 1:
+                total[:, columns] = term
+            else:
+                delta = term.astype(jnp.bfloat16).astype(jnp.float32)
+                out[:, columns] = (base_v[:, columns].astype(jnp.float32) + delta).astype(jnp.bfloat16)
+
+        @pl.loop(0, D // 512)
+        def _(step):
+            add(0, pl.ds(pl.multiple_of(step * 512, 512), 512))
+
+        for which in (1, 2):
+
+            @pl.loop(0, KVW // 512)
+            def _(step):
+                add(which, pl.ds(pl.multiple_of(D + (which - 1) * KVW + step * 512, 512), 512))
+
+    def relay_z(distance):
         for up in (0, 1):
             zz = z - distance if up else z + distance
             inside = zz >= 0 if up else zz < Z
@@ -193,76 +261,54 @@
                 to_x(zz, y).start()
                 to_core(zz, y, x).start()
 
-    for turn in range(Z):
-        zz = (z + turn) % Z
+    def relay_y(g):
+        zz = planes[g]
         arrived(index(zz, 1 - y, c), x)
         to_x(zz, 1 - y).start()
         to_core(zz, 1 - y, x).start()
 
-    for turn in range(Z):
-        zz = (z + turn) % Z
-        for yy in (y, 1 - y):
-            if turn == 0 and yy is y:
-                continue
+    def relay_x(g):
+        zz = planes[g]
+        for yy in (1 - y,) if g == 0 else (y, 1 - y):
             arrived(index(zz, yy, c), 1 - x)
             to_core(zz, yy, 1 - x).start()
 
+    own = pltpu.make_async_copy(block(outgoing, 0, at), block(incoming, 0, at), local_sem.at[5])
+    own.start()
+    relay_z(1)
+    relay_z(2)
+    send_rows(1, True)
+    relay_z(3)
+    send_rows(3, True)
+    send_rows(2, True)
+    send_rows(0, True)
+    relay_y(0)
+    relay_y(1)
+    relay_y(2)
+    relay_y(3)
+    send_rows(1, False)
+    send_rows(0, False)
+    send_rows(3, False)
+    send_rows(2, False)
+    relay_x(0)
     loads[3].wait()
     own.wait()
-    for k in range(1, PEERS):
-        row_copy(k).wait_recv()
-
-    acc[...] = jnp.zeros_like(acc)
-
-    @pl.loop(0, D // 1024)
-    def _(step):
-        part = pl.ds(pl.multiple_of(step * 1024, 1024), 1024)
-        acc[...] += jnp.dot(incoming[:, part], shrink_v[part, :], preferred_element_type=jnp.float32)
-
-    from_at = lax.broadcasted_iota(jnp.int32, (3 * R, 6 * R), 0)
-    to_at = lax.broadcasted_iota(jnp.int32, (3 * R, 6 * R), 1)
-    block_of = jnp.where(from_at >= R, 1, 0) + jnp.where(from_at >= 2 * R, 1, 0)
-    spread = jnp.where(to_at == from_at + R * block_of + R * c, 1.0, 0.0).astype(jnp.bfloat16)
-    lat_out[...] = jnp.dot(
-        acc[...].astype(jnp.bfloat16), spread, preferred_element_type=jnp.float32
-    ).astype(jnp.bfloat16)
-
-    for k in range(1, PEERS):
-        latent_copy(k).start()
-    own_slots = pl.ds(pl.multiple_of(me * CAP, CAP), CAP)
-    lat_in[own_slots, :] = lat_out[own_slots, :]
-
-    for zz in range(Z):
-        for yy in range(Y):
-            for h in range(2):
-                arrived(index(zz, yy, 1 - c), h)
+    serve(0)
+    relay_x(1)
+    serve(1)
+    relay_x(2)
+    relay_x(3)
     loads[4].wait()
-    for k in range(1, PEERS):
-        latent_copy(k).wait_recv()
-
-    for pair in range(PEERS // 2):
-        slots = slice(pair * 2 * CAP, (pair + 1) * 2 * CAP)
-        got = jnp.dot(taker[:, slots], lat_in[slots, :], preferred_element_type=jnp.float32).astype(jnp.bfloat16)
-        for which in range(3):
-            lat3[which, :, pair * 128 : (pair + 1) * 128] = got[:, which * 128 : (which + 1) * 128]
-
-    def finish(which, columns):
-        delta = jnp.dot(lat3[which], wg[:, columns], preferred_element_type=jnp.float32).astype(jnp.bfloat16)
-        out[:, columns] = (base_v[:, columns].astype(jnp.float32) + delta.astype(jnp.float32)).astype(jnp.bfloat16)
-
-    @pl.loop(0, D // 512)
-    def _(step):
-        finish(0, pl.ds(pl.multiple_of(step * 512, 512), 512))
-
-    for which in (1, 2):
-
-        @pl.loop(0, KVW // 512)
-        def _(step, which=which):
-            finish(which, pl.ds(pl.multiple_of(D + (which - 1) * KVW + step * 512, 512), 512))
-
-    for k in range(1, PEERS):
-        row_copy(k).wait_send()
-        latent_copy(k).wait_send()
+    add_plane(0)
+    add_plane(1)
+    serve(2)
+    serve(3)
+    add_plane(2)
+    add_plane(3)
+    for g in range(Z):
+        for j in others(g):
+            row_copy(g, j).wait_send()
+            latent_copy(g, j).wait_send()
     for zz in range(Z):
 
         @pl.when((z < Z - 1) & (zz <= z))
@@ -281,9 +327,6 @@
             @pl.when((zz != z) | (yy != y))
             def _(zz=zz, yy=yy):
                 to_x(zz, yy).wait_send()
-
-
-ORDER = tuple(range(1, PEERS))
 
 
 def gathered(hidden, base_qkv, adapter_id, shrink, expand_q, expand_kv):
@@ -293,18 +336,19 @@
     return pl.pallas_call(
         exchange,
         out_shape=jax.ShapeDtypeStruct((ROW_DEV, QKV), bf16),
-        in_specs=[vmem, vmem, vmem, anywhere, anywhere, anywhere, anywhere],
+        in_specs=[vmem, vmem, anywhere, anywhere, anywhere, anywhere],
         out_specs=vmem,
         scratch_shapes=[
             pltpu.VMEM((PEERS * R, QKV), bf16),
             pltpu.VMEM((SLOTS, D), bf16),
             pltpu.VMEM((SLOTS, D), bf16),
-            pltpu.VMEM((D, 3 * R), bf16),
+            pltpu.VMEM((3 * R, D), bf16),
             pltpu.VMEM((ROW_DEV, QKV), bf16),
-            pltpu.VMEM((SLOTS, 3 * R), jnp.float32),
+            pltpu.VMEM((4 * CAP, 3 * R), jnp.float32),
             pltpu.VMEM((SLOTS, 6 * R), bf16),
             pltpu.VMEM((SLOTS, 6 * R), bf16),
-            pltpu.VMEM((3, ROW_DEV, PEERS * R), bf16),
+            pltpu.VMEM((3, ROW_DEV, 4 * R), bf16),
+            pltpu.VMEM((ROW_DEV, QKV), jnp.float32),
             dma((6,)),
             dma((PEERS,)),
             dma((PEERS,)),
@@ -320,7 +364,9 @@
             collective_id=0, has_side_effects=True, vmem_limit_bytes=56 * 1024 * 1024
         ),
         cost_estimate=pl.CostEstimate(flops=4 * 10**9, bytes_accessed=12 * 10**6, transcendentals=0),
-    )(adapter_id.reshape(1, ROW_DEV), adapter_id, hidden, base_qkv, shrink, expand_q, expand_kv)
+    )(
+        adapter_id.reshape(1, ROW_DEV), hidden, base_qkv, jnp.swapaxes(shrink, 1, 2), expand_q, expand_kv
+    )
 
 
 def fits(mesh, hidden, shrink, expand_q):

time: 242 us -> 162 us (0.67)
  Pallas kernels: 230 us -> 158 us
  local copies, waits for them, and re-layouts: 10.8 us -> 3.46 us
    pallas_call x1, Pallas kernels: 230 us -> 158 us  [gathered(): pl.pallas_call(exchange, out_shape=jax.ShapeDtypeStruct((ROW_DEV, QKV), b...]
    unnamed x3 -> x1, local copies, waits for them, and re-layouts: 10.8 us -> 3.46 us
where the time goes in v2:
time: 162 us
  Pallas kernels  158 us (98%)
  local copies, waits for them, and re-layouts  3.46 us (2%)
    pallas_call x1, Pallas kernels, gathered(): pl.pallas_call(exchange, out_shape=jax.ShapeDtypeStruct((ROW_DEV, QKV), b...  158 us
    unnamed x1, local copies, waits for them, and re-layouts  3.46 us

profile of v2, /device:TPU:0, one launch (start us, length us, event | category | flops | bytes accessed | tf_op | source)
XLA Modules:
  0.0 161.8 jit_solution(197390551449840557)
XLA Ops:
  0.0 158.3 %shard_map.64 = bf16[128,10240]{1,0:T(8,128)(2,1)} custom-call(s32[1,128]{1,0:T(1,128)} %bitcast.3, bf16[128,8192]{1,0:T(8,128)(2,1)} %hidden.1, bf16[128,10240]{1,0:T(8,128)(2,1)} %base.1, bf16[1,192,8192]{2,1,0:T(8,128)(2,1)} %bitcast.2, bf16[1,64,8192]{2,1,0:T(8,128)(2,1)} %expand_q.1, bf16[1,2,64,1024]{3,2,1,0:T(8,128)(2,1)} %expand_kv.1), custom_call_target="tpu_custom_call" | custom-call | flops 4000000000 | bytes 12000000 | tf_op jit(solution)/shard_map/pallas_call | solution.py:336
  158.3 3.5 %copy.8 = bf16[128,10240]{1,0:T(8,128)(2,1)} copy(bf16[128,10240]{1,0:T(8,128)(2,1)} %shard_map.64) | data formatting | bytes 5242880

commit v3 on v2

--- a/solution.py
+++ b/solution.py
@@ -57,6 +57,7 @@
 KVW = 1024
 QKV = D + 2 * KVW
 HALF = R // 2
+WIDE = 1024
 SLOTS = PEERS * CAP
 MESH = pl.DeviceIdType.MESH
 
@@ -186,15 +187,16 @@
             if (j < 2) == near:
                 row_copy(g, j).start()
 
-    def serve(g):
-        for j in others(g):
-            row_copy(g, j).wait_recv()
-        span = slice(g * 4 * CAP, (g + 1) * 4 * CAP)
+    def serve(*pair):
+        for g in pair:
+            for j in others(g):
+                row_copy(g, j).wait_recv()
+        span = slice(pair[0] * 4 * CAP, (pair[-1] + 1) * 4 * CAP)
         latents[...] = jnp.zeros_like(latents)
 
-        @pl.loop(0, D // 1024)
+        @pl.loop(0, D // 2048)
         def _(step):
-            part = pl.ds(pl.multiple_of(step * 1024, 1024), 1024)
+            part = pl.ds(pl.multiple_of(step * 2048, 2048), 2048)
             latents[...] += lax.dot_general(
                 incoming[span, part], shrink_v[:, part], (((1,), (1,)), ((), ())),
                 preferred_element_type=jnp.float32,
@@ -203,45 +205,52 @@
         lat_out[span, :] = jnp.dot(
             latents[...].astype(jnp.bfloat16), spread, preferred_element_type=jnp.float32
         ).astype(jnp.bfloat16)
-        for j in others(g):
-            latent_copy(g, j).start()
-        if g == 0:
+        for g in pair:
+            for j in others(g):
+                latent_copy(g, j).start()
+        if pair[0] == 0:
             own_slots = pl.ds(pl.multiple_of(at * CAP, CAP), CAP)
             lat_in[own_slots, :] = lat_out[own_slots, :]
 
-    def add_plane(g):
-        for yy in range(Y):
-            for h in range(2):
-                arrived(index(planes[g], yy, 1 - c), h)
-        for j in others(g):
-            latent_copy(g, j).wait_recv()
-        for pair in range(2):
-            slots = slice((2 * g + pair) * 2 * CAP, (2 * g + pair + 1) * 2 * CAP)
-            got = jnp.dot(taker[:, slots], lat_in[slots, :], preferred_element_type=jnp.float32)
-            got = got.astype(jnp.bfloat16)
-            for which in range(3):
-                lat3[which, :, pair * 128 : (pair + 1) * 128] = got[:, which * 128 : (which + 1) * 128]
-        rows = pl.ds(pl.multiple_of(planes[g] * 4 * R, 4 * R), 4 * R)
+    def add_planes(*pair):
+        for g in pair:
+            for yy in range(Y):
+                for h in range(2):
+                    arrived(index(planes[g], yy, 1 - c), h)
+        for g in pair:
+            for j in others(g):
+                latent_copy(g, j).wait_recv()
+            for two in range(2):
+                slots = slice((2 * g + two) * 2 * CAP, (2 * g + two + 1) * 2 * CAP)
+                got = jnp.dot(taker[:, slots], lat_in[slots, :], preferred_element_type=jnp.float32)
+                got = got.astype(jnp.bfloat16)
+                lane = (g - pair[0]) * 256 + two * 128
+                for which in range(3):
+                    lat3[which, :, lane : lane + 128] = got[:, which * 128 : (which + 1) * 128]
 
         def add(which, columns):
-            term = jnp.dot(lat3[which], wg[rows, columns], preferred_element_type=jnp.float32)
-            if g > 0:
+            term = None
+            for i, g in enumerate(pair):
+                rows = pl.ds(pl.multiple_of(planes[g] * 4 * R, 4 * R), 4 * R)
+                product = jnp.dot(
+                    lat3[which, :, i * 256 : (i + 1) * 256], wg[rows, columns],
+                    preferred_element_type=jnp.float32,
+                )
+                term = product if term is None else term + product
+            if pair[0] > 0:
                 term += total[:, columns]
-            if g < Z - 1:
+            if pair[-1] < Z - 1:
                 total[:, columns] = term
             else:
                 delta = term.astype(jnp.bfloat16).astype(jnp.float32)
                 out[:, columns] = (base_v[:, columns].astype(jnp.float32) + delta).astype(jnp.bfloat16)
 
-        @pl.loop(0, D // 512)
+        @pl.loop(0, D // WIDE)
         def _(step):
-            add(0, pl.ds(pl.multiple_of(step * 512, 512), 512))
-
-        for which in (1, 2):
-
-            @pl.loop(0, KVW // 512)
-            def _(step):
-                add(which, pl.ds(pl.multiple_of(D + (which - 1) * KVW + step * 512, 512), 512))
+            add(0, pl.ds(pl.multiple_of(step * WIDE, WIDE), WIDE))
+
+        add(1, slice(D, D + KVW))
+        add(2, slice(D + KVW, QKV))
 
     def relay_z(distance):
         for up in (0, 1):
@@ -293,18 +302,14 @@
     relay_x(0)
     loads[3].wait()
     own.wait()
-    serve(0)
+    serve(0, 1)
     relay_x(1)
-    serve(1)
+    loads[4].wait()
+    add_planes(0, 1)
     relay_x(2)
     relay_x(3)
-    loads[4].wait()
-    add_plane(0)
-    add_plane(1)
-    serve(2)
-    serve(3)
-    add_plane(2)
-    add_plane(3)
+    serve(2, 3)
+    add_planes(2, 3)
     for g in range(Z):
         for j in others(g):
             row_copy(g, j).wait_send()
@@ -344,10 +349,10 @@
             pltpu.VMEM((SLOTS, D), bf16),
             pltpu.VMEM((3 * R, D), bf16),
             pltpu.VMEM((ROW_DEV, QKV), bf16),
-            pltpu.VMEM((4 * CAP, 3 * R), jnp.float32),
+            pltpu.VMEM((8 * CAP, 3 * R), jnp.float32),
             pltpu.VMEM((SLOTS, 6 * R), bf16),
             pltpu.VMEM((SLOTS, 6 * R), bf16),
-            pltpu.VMEM((3, ROW_DEV, 4 * R), bf16),
+            pltpu.VMEM((3, ROW_DEV, PEERS * R), bf16),
             pltpu.VMEM((ROW_DEV, QKV), jnp.float32),
             dma((6,)),
             dma((PEERS,)),

time: 162 us -> 153 us (0.944)
  Pallas kernels: 158 us -> 149 us
    pallas_call x1, Pallas kernels: 158 us -> 149 us  [gathered(): pl.pallas_call(exchange, out_shape=jax.ShapeDtypeStruct((ROW_DEV, QKV), b...]
where the time goes in v3:
time: 153 us
  Pallas kernels  149 us (97%)
  local copies, waits for them, and re-layouts  3.46 us (2%)
    pallas_call x1, Pallas kernels, gathered(): pl.pallas_call(exchange, out_shape=jax.ShapeDtypeStruct((ROW_DEV, QKV), b...  149 us
    unnamed x1, local copies, waits for them, and re-layouts  3.46 us

profile of v3, /device:TPU:0, one launch (start us, length us, event | category | flops | bytes accessed | tf_op | source)
XLA Modules:
  0.0 152.9 jit_solution(14996065624690508054)
XLA Ops:
  0.0 149.4 %shard_map.64 = bf16[128,10240]{1,0:T(8,128)(2,1)} custom-call(s32[1,128]{1,0:T(1,128)} %bitcast.3, bf16[128,8192]{1,0:T(8,128)(2,1)} %hidden.1, bf16[128,10240]{1,0:T(8,128)(2,1)} %base.1, bf16[1,192,8192]{2,1,0:T(8,128)(2,1)} %bitcast.2, bf16[1,64,8192]{2,1,0:T(8,128)(2,1)} %expand_q.1, bf16[1,2,64,1024]{3,2,1,0:T(8,128)(2,1)} %expand_kv.1), custom_call_target="tpu_custom_call" | custom-call | flops 4000000000 | bytes 12000000 | tf_op jit(solution)/shard_map/pallas_call | solution.py:341
  149.4 3.5 %copy.8 = bf16[128,10240]{1,0:T(8,128)(2,1)} copy(bf16[128,10240]{1,0:T(8,128)(2,1)} %shard_map.64) | data formatting | bytes 5242880

commit v4 on v3

--- a/solution.py
+++ b/solution.py
@@ -63,9 +63,9 @@
 
 
 def exchange(
-    id_row, hidden, base, shrink, expand_q, expand_kv, out,
-    wg, outgoing, incoming, shrink_v, base_v, latents, lat_out, lat_in, lat3, total,
-    local_sem, p_send, p_recv, l_send, l_recv, w_recv, z_send, y_send, x_send, c_send,
+    id_row, hidden_in, base, shrink, expand_q, expand_kv, result,
+    wg, outgoing, incoming, shrink_v, base_v, latents, lat_out, lat_in, lat3, total, hidden, out,
+    local_sem, p_send, p_recv, l_send, l_recv, w_recv, z_send, y_send, x_send, c_send, out_sem,
 ):
     x = lax.axis_index("group")
     me = lax.axis_index("adapter")
@@ -83,6 +83,7 @@
         pltpu.make_async_copy(expand_kv.at[0, 1], wg.at[own_rows, D + KVW : QKV], local_sem.at[2]),
         pltpu.make_async_copy(shrink.at[0], shrink_v, local_sem.at[3]),
         pltpu.make_async_copy(base, base_v, local_sem.at[4]),
+        pltpu.make_async_copy(hidden_in, hidden, local_sem.at[6]),
     ]
     for load in loads:
         load.start()
@@ -155,6 +156,8 @@
     block_of = jnp.where(from_at >= R, 1, 0) + jnp.where(from_at >= 2 * R, 1, 0)
     spread = jnp.where(to_at == from_at + R * block_of + R * c, 1.0, 0.0).astype(jnp.bfloat16)
 
+    loads[5].wait()
+
     @pl.loop(0, D // 1024)
     def _(step):
         columns = pl.ds(pl.multiple_of(step * 1024, 1024), 1024)
@@ -211,6 +214,10 @@
         if pair[0] == 0:
             own_slots = pl.ds(pl.multiple_of(at * CAP, CAP), CAP)
             lat_in[own_slots, :] = lat_out[own_slots, :]
+
+    def store(step):
+        columns = pl.ds(pl.multiple_of(step * WIDE, WIDE), WIDE)
+        return pltpu.make_async_copy(out.at[:, columns], result.at[:, columns], out_sem.at[step])
 
     def add_planes(*pair):
         for g in pair:
@@ -248,9 +255,14 @@
         @pl.loop(0, D // WIDE)
         def _(step):
             add(0, pl.ds(pl.multiple_of(step * WIDE, WIDE), WIDE))
+            if pair[-1] == Z - 1:
+                store(step).start()
 
         add(1, slice(D, D + KVW))
         add(2, slice(D + KVW, QKV))
+        if pair[-1] == Z - 1:
+            for step in range(D // WIDE, QKV // WIDE):
+                store(step).start()
 
     def relay_z(distance):
         for up in (0, 1):
@@ -310,6 +322,8 @@
     relay_x(3)
     serve(2, 3)
     add_planes(2, 3)
+    for step in range(QKV // WIDE):
+        store(step).wait()
     for g in range(Z):
         for j in others(g):
             row_copy(g, j).wait_send()
@@ -341,8 +355,8 @@
     return pl.pallas_call(
         exchange,
         out_shape=jax.ShapeDtypeStruct((ROW_DEV, QKV), bf16),
-        in_specs=[vmem, vmem, anywhere, anywhere, anywhere, anywhere],
-        out_specs=vmem,
+        in_specs=[vmem, anywhere, anywhere, anywhere, anywhere, anywhere],
+        out_specs=anywhere,
         scratch_shapes=[
             pltpu.VMEM((PEERS * R, QKV), bf16),
             pltpu.VMEM((SLOTS, D), bf16),
@@ -354,7 +368,9 @@
             pltpu.VMEM((SLOTS, 6 * R), bf16),
             pltpu.VMEM((3, ROW_DEV, PEERS * R), bf16),
             pltpu.VMEM((ROW_DEV, QKV), jnp.float32),
-            dma((6,)),
+            pltpu.VMEM((ROW_DEV, D), bf16),
+            pltpu.VMEM((ROW_DEV, QKV), bf16),
+            dma((7,)),
             dma((PEERS,)),
             dma((PEERS,)),
             dma((PEERS,)),
@@ -364,6 +380,7 @@
             dma((Z,)),
             dma((Z, Y)),
             dma((Z, Y, 2)),
+            dma((QKV // WIDE,)),
         ],
         compiler_params=pltpu.CompilerParams(
             collective_id=0, has_side_effects=True, vmem_limit_bytes=56 * 1024 * 1024

time: 153 us -> 151 us (0.987)
    pallas_call x1, Pallas kernels: 149 us -> 148 us  [gathered(): pl.pallas_call(exchange, out_shape=jax.ShapeDtypeStruct((ROW_DEV, QKV), b...]
where the time goes in v4:
time: 151 us
  Pallas kernels  148 us (98%)
  local copies, waits for them, and re-layouts  3.46 us (2%)
    pallas_call x1, Pallas kernels, gathered(): pl.pallas_call(exchange, out_shape=jax.ShapeDtypeStruct((ROW_DEV, QKV), b...  148 us
    unnamed x1, local copies, waits for them, and re-layouts  3.46 us

profile of v4, /device:TPU:0, one launch (start us, length us, event | category | flops | bytes accessed | tf_op | source)
XLA Modules:
  0.0 151.3 jit_solution(14097365901816228553)
XLA Ops:
  0.0 147.9 %shard_map.64 = bf16[128,10240]{1,0:T(8,128)(2,1)} custom-call(s32[1,128]{1,0:T(1,128)} %bitcast.3, bf16[128,8192]{1,0:T(8,128)(2,1)} %hidden_in.1, bf16[128,10240]{1,0:T(8,128)(2,1)} %base.1, bf16[1,192,8192]{2,1,0:T(8,128)(2,1)} %bitcast.2, bf16[1,64,8192]{2,1,0:T(8,128)(2,1)} %expand_q.1, bf16[1,2,64,1024]{3,2,1,0:T(8,128)(2,1)} %expand_kv.1), custom_call_target="tpu_custom_call" | custom-call | flops 4000000000 | bytes 12000000 | tf_op jit(solution)/shard_map/pallas_call | solution.py:355
  147.9 3.5 %copy.8 = bf16[128,10240]{1,0:T(8,128)(2,1)} copy(bf16[128,10240]{1,0:T(8,128)(2,1)} %shard_map.64) | data formatting | bytes 5242880
